TPU v7x, 32 devices: a whole 2x2x4 slice. The times are simulated.
32 devices in a mesh: head: 4 (over y, core), req: 8 (over z, x).
Axes of the slice: x: 2, y: 2, z: 4, core: 2. Of those that a mesh axis runs over, the one named last changes fastest.
Arguments:
- learner_acceptance_matrix: float32 [2048, 2048], P(('head', 'req')), may hold values from -0.125 to 0.125
- learner_address_matrix: float32 [2048, 2048], P(('head', 'req')), may hold values from -0.125 to 0.125
- learner_content_matrix: float32 [2048, 2048], P(('head', 'req')), may hold values from -0.125 to 0.125
- learner_gating_matrix: float32 [2048, 2048], P(('head', 'req')), may hold values from -0.125 to 0.125
- learner_result_matrix: float32 [2048, 2048], P(('head', 'req')), may hold values from -0.125 to 0.125
- fading_narrowing_matrix: bfloat16 [2048, 64], replicated, may hold values from -0.125 to 0.125
- fading_widening_matrix: bfloat16 [64, 2048], P(None, 'head'), may hold values from -0.75 to 0.75
- feature_fading_speed: float32 [2048], P('head'), may hold values from 0.001 to 0.5
- current_reward: float32 [2048], P('head'), may hold values from -1 to 1
- symbol_blending_factors: float32 [5, 2048], replicated, may hold values from 0 to 1
- group_scaling_factor: float32 [2048], P('head'), may hold values from 0.5 to 1.5
- group_scaling_offset: float32 [2048], P('head'), may hold values from -1.75 to 1.75
- request_hidden_entries: bfloat16 [16, 512, 2048], P('req', None, 'head'), may hold values from -6 to 6
- request_valid_count: int32 [16], P('req'), may hold values from 1 to 512, 6144 in all
- request_destination_place: int32 [16], P('req'), may hold values from 0 to 511, as said below
- newest_symbol_hidden: bfloat16 [512, 2048], P('req', 'head'), may hold values from -6 to 6
- preceding_hidden_entry: bfloat16 [512, 2048], P('req', 'head'), may hold values from -6 to 6
- place_memory_matrix: float32 [512, 32, 64, 64], P('req', 'head'), may hold values from -6 to 6
- place_newness_marks: int32 [512], P('req'), may hold values 0 or 1
Outputs:
- prompt_hidden: bfloat16 [16, 512, 2048], P('req', None, 'head')
- decode_hidden: bfloat16 [512, 2048], P('req', 'head')
- new_state: float32 [512, 32, 64, 64], P('req', 'head')
- new_shift: bfloat16 [512, 2048], P('req', 'head')
Inputs may be any that keep to these rules, and one draw needn't show every extreme that they name: Prompt p's slot is one of the 64 slots of the same index of req as prompt p, that is p // 2 == request_destination_place[p] // 64; the slots are distinct. `request_valid_count`: the longest prompt has exactly 512 live tokens.
All inputs are finite; a program needn't handle non-finite values. No bound on the sum of `request_valid_count` or of `place_newness_marks` on one device may be relied on, other than what follows from the above.
Results may differ from a plain program's by a relative error of at most 0.033.
Values may be sent and summed in bfloat16 or wider, within the bound.
A program may use at most 256 MiB of HBM per device.

v0:
```python
import functools

import jax
import jax.numpy as jnp
from jax import lax
from jax.experimental import pallas as pl
from jax.experimental.pallas import tpu as pltpu
from jax.sharding import PartitionSpec as P

NORM_EPS = 0.00064
VMEM_LIMIT = 50 * 1024 * 1024


def project(left, right):
    return jnp.dot(left, right, preferred_element_type=jnp.float32)


def contract(left, right, left_dim, right_dim):
    return lax.dot_general(
        left, right, (((left_dim,), (right_dim,)), ((), ())), preferred_element_type=jnp.float32
    )


MESH = pl.DeviceIdType.MESH


def mixed_tokens(current, newest, prior, mix, length):
    current = current.astype(jnp.float32)
    row = lax.broadcasted_iota(jnp.int32, current.shape, 0)
    shifted = jnp.where(row % length == 0, 0.0, pltpu.roll(current, 1, 0))
    newest = newest.astype(jnp.float32)
    prior = prior.astype(jnp.float32)
    return (
        (current + (shifted - current) * mix).astype(jnp.bfloat16),
        (newest + (prior - newest) * mix).astype(jnp.bfloat16),
    )


def gather_project_kernel(
    features_ref,
    shards_ref,
    mix_ref,
    narrow_ref,
    widen_ref,
    speed_ref,
    live_ref,
    k_ref,
    v_ref,
    r_ref,
    w_ref,
    g_ref,
    features,
    weights,
    acc,
    low_acc,
    local_sem,
    turn_send,
    turn_recv,
    feature_send,
    feature_recv,
    outer_send,
    outer_recv,
    inner_send,
    inner_recv,
    *,
    prompt_rows,
    length,
    n_head,
    n_req,
):
    matrices = weights.shape[0]
    head = lax.axis_index("head")
    req = lax.axis_index("req")
    n_outer = n_req // 2
    partner = req + 1 - 2 * (req % 2)
    sibling = head + 1 - 2 * (head % 2)
    across = (head + n_head // 2) % n_head
    slots = (features.shape[1] - prompt_rows) // 2

    barrier = pltpu.get_barrier_semaphore()
    for d in range(1, n_head):
        pl.semaphore_signal(
            barrier, inc=1, device_id={"head": (head + d) % n_head}, device_id_type=MESH
        )
    for d in range(1, n_outer):
        pl.semaphore_signal(
            barrier, inc=1, device_id={"req": (req + 2 * d) % n_req}, device_id_type=MESH
        )
    pl.semaphore_signal(barrier, inc=1, device_id={"req": partner}, device_id_type=MESH)
    pl.semaphore_wait(barrier, n_head - 1 + n_outer)

    def turn(d):
        target = (head + d) % n_head
        return pltpu.make_async_remote_copy(
            src_ref=shards_ref.at[target],
            dst_ref=weights.at[:, req, head],
            send_sem=turn_send.at[d - 1],
            recv_sem=turn_recv.at[d - 1],
            device_id={"head": target},
            device_id_type=MESH,
        )

    def feature(block, src, target, number):
        return pltpu.make_async_remote_copy(
            src_ref=src,
            dst_ref=features.at[block],
            send_sem=feature_send.at[number],
            recv_sem=feature_recv.at[number],
            device_id={"head": target},
            device_id_type=MESH,
        )

    def outer(m, d):
        return pltpu.make_async_remote_copy(
            src_ref=weights.at[m, req],
            dst_ref=weights.at[m, req],
            send_sem=outer_send.at[m, d - 1],
            recv_sem=outer_recv.at[m, d - 1],
            device_id={"req": (req + 2 * d) % n_req},
            device_id_type=MESH,
        )

    def inner(m, d):
        block = (req - 2 * d + n_req) % n_req
        return pltpu.make_async_remote_copy(
            src_ref=weights.at[m, block],
            dst_ref=weights.at[m, block],
            send_sem=inner_send.at[m, d],
            recv_sem=inner_recv.at[m, d],
            device_id={"req": partner},
            device_id_type=MESH,
        )

    def arrived_outer(m, d):
        block = (req - 2 * d + n_req) % n_req
        pltpu.make_async_remote_copy(
            src_ref=weights.at[m, block],
            dst_ref=weights.at[m, block],
            send_sem=outer_send.at[m, d - 1],
            recv_sem=outer_recv.at[m, d - 1],
            device_id={"req": (req + 2 * d) % n_req},
            device_id_type=MESH,
        ).wait_recv()

    def arrived_inner(m, d):
        block = (partner - 2 * d + n_req) % n_req
        pltpu.make_async_remote_copy(
            src_ref=weights.at[m, block],
            dst_ref=weights.at[m, block],
            send_sem=inner_send.at[m, d],
            recv_sem=inner_recv.at[m, d],
            device_id={"req": partner},
            device_id_type=MESH,
        ).wait_recv()

    own_turn = pltpu.make_async_copy(
        shards_ref.at[head], weights.at[:, req, head], local_sem.at[0]
    )
    own_turn.start()
    for d in range(1, n_head):
        turn(d).start()
    to_across = feature(head, features_ref, across, 0)
    to_across.start()
    to_sibling = feature(head, features_ref, sibling, 1)
    to_sibling.start()
    own_features = pltpu.make_async_copy(features_ref, features.at[head], local_sem.at[1])
    own_features.start()

    own_turn.wait()
    for d in range(1, n_head):
        source = (head - d + n_head) % n_head
        pltpu.make_async_remote_copy(
            src_ref=shards_ref.at[source],
            dst_ref=weights.at[:, req, source],
            send_sem=turn_send.at[d - 1],
            recv_sem=turn_recv.at[d - 1],
            device_id={"head": source},
            device_id_type=MESH,
        ).wait_recv()
    for m in range(matrices):
        inner(m, 0).start()
        for d in range(1, n_outer):
            outer(m, d).start()

    feature(across, features_ref, across, 0).wait_recv()
    passed_on = feature(across, features.at[across], sibling, 2)
    passed_on.start()
    feature(sibling, features_ref, sibling, 1).wait_recv()
    own_features.wait()
    far = (sibling + n_head // 2) % n_head
    feature(far, features.at[far], sibling, 2).wait_recv()

    def multiply(number, weight_of, total):
        total[...] = jnp.zeros_like(total)

        @pl.loop(0, n_head)
        def _(h):
            prompts, newest = mixed_tokens(
                features[h, :prompt_rows],
                features[h, prompt_rows : prompt_rows + slots],
                features[h, prompt_rows + slots :],
                mix_ref[number, h],
                length,
            )
            weight = weight_of(h)
            total[:prompt_rows] += project(prompts, weight)
            total[prompt_rows:] += project(newest, weight)

    def forward(m):
        for d in range(1, n_outer):
            arrived_outer(m, d)
            inner(m, d).start()

    def gathered(m):
        def weight_of(h):
            return weights[m, :, h].reshape(-1, weights.shape[-1])

        return weight_of

    def landed(m):
        for d in range(n_outer):
            arrived_inner(m, d)

    multiply(3, lambda h: narrow_ref[h], low_acc)
    lowrank = jnp.tanh(low_acc[...]).astype(jnp.bfloat16)
    w_ref[...] = -speed_ref[...] * jnp.exp(project(lowrank, widen_ref[...])) * live_ref[...]

    forward(0)
    landed(0)
    for m, number in ((0, 1), (1, 2), (2, 0), (3, 4)):
        if m + 1 < matrices:
            forward(m + 1)
        multiply(number, gathered(m), acc)
        if m == 0:
            k_ref[...] = (acc[...] * live_ref[...]).astype(k_ref.dtype)
        elif m == 1:
            v_ref[...] = acc[...].astype(v_ref.dtype)
        elif m == 2:
            r_ref[...] = acc[...].astype(r_ref.dtype)
        else:
            u = acc[...]
            g_ref[...] = u / (1.0 + jnp.exp(-u))
        if m + 1 < matrices:
            landed(m + 1)

    for d in range(1, n_head):
        turn(d).wait_send()
    to_across.wait_send()
    to_sibling.wait_send()
    passed_on.wait_send()
    for m in range(matrices):
        for d in range(1, n_outer):
            outer(m, d).wait_send()
        for d in range(n_outer):
            inner(m, d).wait_send()


def gather_project(features, shards, mix, narrow, widen, speed, live, prompt_rows, length, n_req):
    n_head, matrices, shard_rows, columns = shards.shape
    all_rows = features.shape[0]
    rows = prompt_rows + (all_rows - prompt_rows) // 2
    n_outer = n_req // 2
    whole = pl.BlockSpec(memory_space=pltpu.VMEM)
    sem = pltpu.SemaphoreType.DMA
    return pl.pallas_call(
        functools.partial(
            gather_project_kernel,
            prompt_rows=prompt_rows,
            length=length,
            n_head=n_head,
            n_req=n_req,
        ),
        out_shape=(
            jax.ShapeDtypeStruct((rows, columns), jnp.bfloat16),
            jax.ShapeDtypeStruct((rows, columns), jnp.bfloat16),
            jax.ShapeDtypeStruct((rows, columns), jnp.bfloat16),
            jax.ShapeDtypeStruct((rows, columns), jnp.float32),
            jax.ShapeDtypeStruct((rows, columns), jnp.float32),
        ),
        in_specs=[whole] * 7,
        out_specs=(whole,) * 5,
        scratch_shapes=[
            pltpu.VMEM((n_head, all_rows, features.shape[1]), jnp.bfloat16),
            pltpu.VMEM((matrices, n_req, n_head, shard_rows, columns), jnp.bfloat16),
            pltpu.VMEM((rows, columns), jnp.float32),
            pltpu.VMEM((rows, narrow.shape[-1]), jnp.float32),
            sem((2,)),
            sem((n_head - 1,)),
            sem((n_head - 1,)),
            sem((3,)),
            sem((3,)),
            sem((matrices, n_outer - 1)),
            sem((matrices, n_outer - 1)),
            sem((matrices, n_outer)),
            sem((matrices, n_outer)),
        ],
        compiler_params=pltpu.CompilerParams(
            vmem_limit_bytes=VMEM_LIMIT, collective_id=0, has_side_effects=True
        ),
        cost_estimate=pl.CostEstimate(
            flops=2 * rows * n_head * features.shape[1] * columns * matrices,
            bytes_accessed=200 * 1024 * 1024,
            transcendentals=0,
        ),
    )(features, shards, mix, narrow, widen, speed, live)


def recurrence_kernel(
    r_ref, k_ref, v_ref, w_ref, g_ref, reward_ref, gain_ref, offset_ref, out_ref, final_ref, memory,
    *, breadth, span
):
    pair = 2 * breadth
    chunk = pl.program_id(1)

    @pl.when(chunk == 0)
    def _():
        memory[...] = jnp.zeros_like(memory)

    row = lax.broadcasted_iota(jnp.int32, (span, pair), 0)
    first_head = lax.broadcasted_iota(jnp.int32, (span, pair), 1) < breadth
    later = lax.broadcasted_iota(jnp.int32, (span, span), 0)
    sooner = lax.broadcasted_iota(jnp.int32, (span, span), 1)
    apart = jnp.where(later > sooner, later ^ sooner, 0)
    same_head = (lax.broadcasted_iota(jnp.int32, (pair, pair), 0) < breadth) == (
        lax.broadcasted_iota(jnp.int32, (pair, pair), 1) < breadth
    )
    ones = jnp.where(same_head, 1.0, 0.0).astype(jnp.bfloat16)

    for index in range(memory.shape[0]):
        cols = slice(index * pair, (index + 1) * pair)
        r = r_ref[:, cols].astype(jnp.float32)
        k = k_ref[:, cols].astype(jnp.float32)
        v16 = v_ref[:, cols]
        v = v16.astype(jnp.float32)
        before = jnp.zeros((span, pair), jnp.float32)
        after = jnp.zeros((span, pair), jnp.float32)
        total = w_ref[:, cols]
        scores_a = jnp.zeros((span, span), jnp.float32)
        scores_b = jnp.zeros((span, span), jnp.float32)
        step = 1
        while step < span:
            second = (row & step) != 0
            factor = jnp.where(second, r, k) * jnp.exp(jnp.where(second, before, after))
            factor16 = factor.astype(jnp.bfloat16)
            factor_a = jnp.where(first_head, factor, 0.0).astype(jnp.bfloat16)
            factor_b = jnp.where(first_head, 0.0, factor).astype(jnp.bfloat16)
            level = (apart >= step) & (apart < 2 * step)
            scores_a = jnp.where(level, contract(factor_a, factor16, 1, 1), scores_a)
            scores_b = jnp.where(level, contract(factor_b, factor16, 1, 1), scores_b)
            partner = jnp.where(second, pltpu.roll(total, step, 0), pltpu.roll(total, span - step, 0))
            before = jnp.where(second, before + partner, before)
            after = jnp.where(second, after, after + partner)
            total = total + partner
            step *= 2
        state = memory[index]
        y = jnp.where(
            first_head,
            project(scores_a.astype(jnp.bfloat16), v16),
            project(scores_b.astype(jnp.bfloat16), v16),
        )
        y += contract((r * jnp.exp(before)).astype(jnp.bfloat16), state.astype(jnp.bfloat16), 1, 1)
        y += project((r * reward_ref[:, cols] * k).astype(jnp.bfloat16), ones) * v
        kept = (k * jnp.exp(after)).astype(jnp.bfloat16)
        memory[index] = state * jnp.exp(total[:1]) + jnp.where(
            same_head, contract(v16, kept, 0, 0), 0.0
        )
        high = y.astype(jnp.bfloat16)
        low = (y - high.astype(jnp.float32)).astype(jnp.bfloat16)
        center = y - (project(high, ones) + project(low, ones)) * (1.0 / breadth)
        spread = project((center * center).astype(jnp.bfloat16), ones) * (1.0 / breadth)
        normed = center * lax.rsqrt(spread + NORM_EPS) * gain_ref[:, cols] + offset_ref[:, cols]
        out_ref[:, cols] = (normed * g_ref[:, cols]).astype(out_ref.dtype)

    @pl.when(chunk == pl.num_programs(1) - 1)
    def _():
        for index in range(memory.shape[0]):
            turned = memory[index].T
            final_ref[0, 2 * index] = turned[:breadth, :breadth]
            final_ref[0, 2 * index + 1] = turned[breadth:, breadth:]


def recurrence(r, k, v, w, g, reward, gain, offset, prompt_count, length, breadth):
    columns = r.shape[1]
    span = min(128, length)
    chunks = length // span
    rows_spec = pl.BlockSpec((span, columns), lambda p, c: (p * chunks + c, 0))
    vector_spec = pl.BlockSpec((1, columns), lambda p, c: (0, 0))
    heads = columns // breadth
    return pl.pallas_call(
        functools.partial(recurrence_kernel, breadth=breadth, span=span),
        grid=(prompt_count, chunks),
        out_shape=(
            jax.ShapeDtypeStruct((prompt_count * length, columns), jnp.bfloat16),
            jax.ShapeDtypeStruct((prompt_count, heads, breadth, breadth), jnp.float32),
        ),
        in_specs=[rows_spec] * 5 + [vector_spec] * 3,
        out_specs=(
            rows_spec,
            pl.BlockSpec((1, heads, breadth, breadth), lambda p, c: (p, 0, 0, 0)),
        ),
        scratch_shapes=[pltpu.VMEM((heads // 2, 2 * breadth, 2 * breadth), jnp.float32)],
        compiler_params=pltpu.CompilerParams(vmem_limit_bytes=VMEM_LIMIT),
        cost_estimate=pl.CostEstimate(
            flops=20 * prompt_count * length * columns * span,
            bytes_accessed=14 * prompt_count * length * columns,
            transcendentals=9 * prompt_count * length * columns,
        ),
    )(r, k, v, w, g, reward, gain, offset)


def group_norm(outputs, group_scaling_factor, group_scaling_offset):
    center = outputs - jnp.mean(outputs, axis=-1, keepdims=True)
    spread = jnp.mean(center * center, axis=-1, keepdims=True)
    normed = (center / jnp.sqrt(spread + NORM_EPS)).reshape(outputs.shape[0], -1)
    return normed * group_scaling_factor + group_scaling_offset


def on_device(
    learner_acceptance_matrix,
    learner_address_matrix,
    learner_content_matrix,
    learner_gating_matrix,
    learner_result_matrix,
    fading_narrowing_matrix,
    fading_widening_matrix,
    feature_fading_speed,
    current_reward,
    symbol_blending_factors,
    group_scaling_factor,
    group_scaling_offset,
    request_hidden_entries,
    request_valid_count,
    request_destination_place,
    newest_symbol_hidden,
    preceding_hidden_entry,
    place_memory_matrix,
    place_newness_marks,
):
    block_cols = feature_fading_speed.shape[0]
    owned_groups = place_memory_matrix.shape[1]
    group_breadth = place_memory_matrix.shape[2]
    slot_count = place_memory_matrix.shape[0]
    prompt_count, length = request_hidden_entries.shape[:2]
    prompt_rows = prompt_count * length
    blocks = lax.axis_size("head")
    fresh_mask = place_newness_marks == 1

    prior = jnp.where(fresh_mask[:, None], jnp.zeros_like(preceding_hidden_entry), preceding_hidden_entry)
    features = jnp.concatenate(
        [request_hidden_entries.reshape(prompt_rows, block_cols), newest_symbol_hidden, prior]
    )
    shard_rows = learner_address_matrix.shape[0]
    shards = jnp.stack(
        [
            matrix.astype(jnp.bfloat16).reshape(shard_rows, blocks, block_cols).transpose(1, 0, 2)
            for matrix in (
                learner_address_matrix,
                learner_content_matrix,
                learner_acceptance_matrix,
                learner_gating_matrix,
            )
        ],
        axis=1,
    )
    w_output = lax.all_gather(learner_result_matrix.astype(jnp.bfloat16), "req", axis=0, tiled=True)

    positions = lax.broadcasted_iota(jnp.int32, (prompt_count, length), 1)
    live_mask = (positions < request_valid_count[:, None]).astype(jnp.float32).reshape(-1, 1)
    live_rows = jnp.concatenate([live_mask, jnp.ones((slot_count, 1), jnp.float32)])
    mix = symbol_blending_factors.reshape(5, blocks, 1, block_cols)
    gain = group_scaling_factor.reshape(1, -1)
    offset = group_scaling_offset.reshape(1, -1)

    address, content, acceptance, log_decay, gates = gather_project(
        features,
        shards,
        mix,
        fading_narrowing_matrix.reshape(blocks, block_cols, -1),
        fading_widening_matrix,
        feature_fading_speed.reshape(1, -1),
        live_rows,
        prompt_rows,
        length,
        lax.axis_size("req"),
    )
    gated_prompts, final_state = recurrence(
        acceptance,
        address,
        content,
        log_decay,
        gates,
        current_reward.reshape(1, -1),
        gain,
        offset,
        prompt_count,
        length,
        group_breadth,
    )

    def slot_heads(array):
        return array[prompt_rows:].astype(jnp.float32).reshape(-1, owned_groups, group_breadth)

    slot_r, slot_k, slot_v, slot_w = [
        slot_heads(array) for array in (acceptance, address, content, log_decay)
    ]
    group_reward = current_reward.reshape(owned_groups, group_breadth)
    begin_state = jnp.where(fresh_mask[:, None, None, None], 0.0, place_memory_matrix)
    decode_out = (
        jnp.sum(slot_r[..., None] * begin_state, axis=2)
        + jnp.sum(slot_r * group_reward * slot_k, axis=-1, keepdims=True) * slot_v
    )
    normed_slots = group_norm(decode_out, group_scaling_factor, group_scaling_offset)
    gated_slots = (normed_slots * gates[prompt_rows:]).astype(jnp.bfloat16)
    partial_sum = project(jnp.concatenate([gated_prompts, gated_slots]), w_output).astype(
        jnp.bfloat16
    )
    partial_sum, slot_k, slot_v, slot_w = lax.optimization_barrier(
        (partial_sum, slot_k, slot_v, slot_w)
    )
    hidden = lax.psum_scatter(partial_sum, "head", scatter_dimension=1, tiled=True)
    new_state = (
        jnp.exp(slot_w)[..., None] * begin_state + slot_k[..., :, None] * slot_v[..., None, :]
    )
    prompt_hidden = (
        (hidden[:prompt_rows].astype(jnp.float32) * live_mask)
        .astype(jnp.bfloat16)
        .reshape(prompt_count, length, block_cols)
    )
    select = (positions == request_valid_count[:, None] - 1).astype(jnp.float32)
    last_tokens = jnp.sum(
        request_hidden_entries.astype(jnp.float32) * select[..., None], axis=1
    ).astype(jnp.bfloat16)
    offsets = request_destination_place - lax.axis_index("req") * slot_count
    slot_ids = lax.broadcasted_iota(jnp.int32, (slot_count,), 0)
    new_shift = newest_symbol_hidden
    prompt_taken = jnp.zeros((slot_count,), jnp.bool_)
    for prompt_index in range(prompt_count):
        slot_hit = slot_ids == offsets[prompt_index]
        new_state = jnp.where(slot_hit[:, None, None, None], final_state[prompt_index], new_state)
        new_shift = jnp.where(slot_hit[:, None], last_tokens[prompt_index], new_shift)
        prompt_taken = prompt_taken | slot_hit
    decode_hidden = jnp.where(
        prompt_taken[:, None], jnp.zeros((), jnp.bfloat16), hidden[prompt_rows:]
    )
    return (prompt_hidden, decode_hidden, new_state, new_shift)


def solution(mesh):
    in_specs = (
        P(("head", "req"), None),
        P(("head", "req"), None),
        P(("head", "req"), None),
        P(("head", "req"), None),
        P(("head", "req"), None),
        P(),
        P(None, "head"),
        P("head"),
        P("head"),
        P(),
        P("head"),
        P("head"),
        P("req", None, "head"),
        P("req"),
        P("req"),
        P("req", "head"),
        P("req", "head"),
        P("req", "head", None, None),
        P("req"),
    )
    out_specs = (
        P("req", None, "head"),
        P("req", "head"),
        P("req", "head", None, None),
        P("req", "head"),
    )
    return jax.shard_map(
        on_device, mesh=mesh, in_specs=in_specs, out_specs=out_specs, check_vma=False
    )
```

profile of v0, /device:TPU:0, one launch (start us, length us, event | category | flops | bytes accessed | tf_op | source)
XLA Modules:
  0.0 275.4 jit_solution(18093915308697861865)
XLA Ops:
  7.2 1.9 convert_element_type.69
  9.9 1.1 convert_element_type.65
  11.0 1.1 convert_element_type.64
  12.2 1.0 reshape.163.mix_ref
  14.1 1.1 pad_maximum_fusion.features_ref
  15.4 148.3 %shard_map.210 = (bf16[1088,512]{1,0:T(8,128)(2,1)S(1)}, bf16[1088,512]{1,0:T(8,128)(2,1)}, bf16[1088,512]{1,0:T(8,128)(2,1)}, f32[1088,512]{1,0:T(8,128)}, f32[1088,512]{1,0:T(8,128)}) custom-call(bf16[1152,512]{1,0:T(8,128)(2,1)} %pad_maximum_fusion.features_ref, bf16[4,4,64,512]{3,2,1,0:T(8,128)(2,1)S(1)} %pad_maximum_fusion.1.shards_ref, ...), custom_call_target="tpu_custom_call" | custom-call | flops 9126805504 | bytes 209715200 | tf_op jit(solution)/shard_map/pallas_call | solution.py:265
  163.7 0.9 slice_convert_fusion.2
  164.7 0.9 slice_convert_fusion
  165.9 8.0 %multiply_reduce_fusion = f32[64,8,64]{2,1,0:T(8,128)S(1)} fusion(f32[64,8,64,64]{3,2,1,0:T(8,128)} %param.36, f32[64,8,64]{2,1,0:T(8,128)S(1)} %reshape.174, pred[64]{0:T(512)(128)(4,1)S(1)} %broadcast_compare_fusion), kind=kLoop, calls=%fused_computation.1 | loop fusion | flops 6258688 | bytes 8650816 | tf_op jit(solution)/shard_map/reduce_sum | solution.py:509
  173.8 0.8 reduce_sum.48
  175.4 0.8 div.20
  176.4 0.8 sub.23
  177.3 0.8 mul.102
  178.0 0.9 slice.43
  179.1 25.7 %shard_map.211 = (bf16[1024,512]{1,0:T(8,128)(2,1)S(1)}, f32[2,8,64,64]{3,2,1,0:T(8,128)S(1)}) custom-call(bf16[1088,512]{1,0:T(8,128)(2,1)S(1)} %copy-done, bf16[1088,512]{1,0:T(8,128)(2,1)S(1)} %get-tuple-element.16.k_ref, bf16[1088,512]{1,0:T(8,128)(2,1)} %get-tuple-element.17.v_ref, f32[1088,512]{1,0:T(8,128)} %get-tuple-element.18.w_ref, ...), custom_call_target="tpu_custom_call" | custom-call | flops 1342177280 | bytes 7340032 | tf_op jit(solution)/shard_map/pallas_call | solution.py:389
  204.9 1.0 copy-done.6
  205.9 1.0 multiply_convert_fusion.1
  206.9 6.5 %convolution_convert_fusion = bf16[1088,2048]{1,0:T(8,128)(2,1)} fusion(bf16[512,2048]{1,0:T(8,128)(2,1)} %all-gather.2.cloned.1.call-done, bf16[64,512]{1,0:T(8,128)(2,1)S(1)} %multiply_convert_fusion.1, bf16[1024,512]{1,0:T(8,128)(2,1)} %copy-done.6), kind=kOutput, calls=%fused_computation.2 | convolution fusion | flops 2286157824 | bytes 7667712 | tf_op jit(solution)/shard_map/dot_general | solution.py:15
  215.2 1.3 iota_compare_fusion.2
  216.9 0.7 select_select_fusion.1
  217.8 17.5 %select_select_fusion = f32[64,8,64,64]{3,2,1,0:T(8,128)} fusion(f32[64,8,64,64]{3,2,1,0:T(8,128)} %param.36, f32[64,8,64]{2,1,0:T(8,128)S(1)} %reshape.171, f32[64,8,64]{2,1,0:T(8,128)S(1)} %reshape.176, f32[64,8,64]{2,1,0:T(8,128)S(1)} %exp.3, f32[8,64,64]{2,1,0:T(8,128)S(1)} %get-tuple-element.29, f32[8,64,64]{2,1,0:T(8,128)S(1)} %get-tuple-element.28, ...), kind=kLoop, calls=%fused_computation | loop fusion | flops 12582912 | bytes 17432768 | tf_op jit(solution)/shard_map/jit(_where)/select_n | solution.py:539
  235.2 29.3 %reduce-scatter.2.cloned.1.call-done = bf16[1088,512]{1,0:T(8,128)(2,1)} async-done(((bf16[1088,2048]{1,0:T(8,128)(2,1)}), bf16[1088,512]{1,0:T(8,128)(2,1)}) %reduce-scatter.2.cloned.1.call-update) | async-done | bytes 1114128 | tf_op jit(solution)/shard_map/reduce_scatter | solution.py:520
  264.5 2.5 multiply_convert_fusion
  267.0 1.5 slice_select_fusion
  (88 shorter events, 5.8 us)
Async XLA Ops:
  7.2 4.9 %copy-start.9 = (f32[64,2048]{1,0:T(8,128)S(1)}, f32[64,2048]{1,0:T(8,128)}, u32[]{:S(2)}) copy-start(f32[64,2048]{1,0:T(8,128)} %param.21) | copy-start | bytes 1572868
  7.2 4.9 %copy-start.10 = (f32[64,2048]{1,0:T(8,128)S(1)}, f32[64,2048]{1,0:T(8,128)}, u32[]{:S(2)}) copy-start(f32[64,2048]{1,0:T(8,128)} %param.20) | copy-start | bytes 1572868
  7.2 6.0 %copy-start.15 = (bf16[2048,64]{0,1:T(8,128)(2,1)S(1)}, bf16[2048,64]{0,1:T(8,128)(2,1)}, u32[]{:S(2)}) copy-start(bf16[2048,64]{0,1:T(8,128)(2,1)} %param.24) | copy-start | bytes 786436
  7.2 199.7 %all-gather.2.cloned.1.call-start = ((), (), s32[]{:S(2)}) async-start(), calls=%async_computation.1 | async-start | bytes 2359296 | tf_op jit(solution)/shard_map/all_gather | solution.py:465
  9.1 4.3 %copy-start.21 = (s32[2]{0:T(128)S(1)}, s32[2]{0:T(128)}, u32[]{:S(2)}) copy-start(s32[2]{0:T(128)} %param.32) | copy-start | bytes 28
  9.2 255.3 %reduce-scatter.2.cloned.1.call-start = ((), (), s32[]{:S(2)}) async-start(), calls=%async_computation.2 | async-start | bytes 5570560 | tf_op jit(solution)/shard_map/reduce_scatter | solution.py:520
  9.9 156.0 %copy-start.19 = (pred[64]{0:T(512)(128)(4,1)}, pred[64]{0:T(512)(128)(4,1)S(1)}, u32[]{:S(2)}) copy-start(pred[64]{0:T(512)(128)(4,1)S(1)} %broadcast_compare_fusion) | copy-start | bytes 196
  10.9 3.0 %copy-start.18 = (bf16[64,512]{1,0:T(8,128)(2,1)S(1)}, bf16[64,512]{1,0:T(8,128)(2,1)}, u32[]{:S(2)}) copy-start(bf16[64,512]{1,0:T(8,128)(2,1)} %param.35) | copy-start | bytes 196612
  12.1 2.0 copy-start.7
  12.1 2.0 copy-start.16
  14.1 1.3 copy-start.4
  14.1 1.2 copy-start.5
  15.4 150.4 %copy-start.3 = (f32[512]{0:T(512)S(1)}, f32[512]{0:T(512)}, u32[]{:S(2)}) copy-start(f32[512]{0:T(512)} %param.27) | copy-start | bytes 6148
  174.6 4.5 %copy-start = (bf16[1088,512]{1,0:T(8,128)(2,1)S(1)}, bf16[1088,512]{1,0:T(8,128)(2,1)}, u32[]{:S(2)}) copy-start(bf16[1088,512]{1,0:T(8,128)(2,1)} %get-tuple-element.15.r_ref) | copy-start | bytes 3342340
  174.6 4.5 %copy-start.1 = (f32[512]{0:T(512)S(1)}, f32[512]{0:T(512)}, u32[]{:S(2)}) copy-start(f32[512]{0:T(512)} %param.30) | copy-start | bytes 6148
  174.6 4.5 %copy-start.2 = (f32[512]{0:T(512)S(1)}, f32[512]{0:T(512)}, u32[]{:S(2)}) copy-start(f32[512]{0:T(512)} %param.29) | copy-start | bytes 6148
  179.1 26.8 %copy-start.11 = (f32[64,512]{1,0:T(8,128)S(1)}, f32[64,512]{1,0:T(8,128)}, u32[]{:S(2)}) copy-start(f32[64,512]{1,0:T(8,128)} %reduce_sum.48) | copy-start | bytes 393220
  179.1 26.8 %copy-start.12 = (f32[64,512]{1,0:T(8,128)S(1)}, f32[64,512]{1,0:T(8,128)}, u32[]{:S(2)}) copy-start(f32[64,512]{1,0:T(8,128)} %div.20) | copy-start | bytes 393220
  179.1 26.7 %copy-start.13 = (f32[64,512]{1,0:T(8,128)S(1)}, f32[64,512]{1,0:T(8,128)}, u32[]{:S(2)}) copy-start(f32[64,512]{1,0:T(8,128)} %sub.23) | copy-start | bytes 393220
  179.1 26.7 %copy-start.14 = (f32[64,512]{1,0:T(8,128)S(1)}, f32[64,512]{1,0:T(8,128)}, u32[]{:S(2)}) copy-start(f32[64,512]{1,0:T(8,128)} %mul.102) | copy-start | bytes 393220
  213.3 3.2 %copy-start.22 = (s32[2]{0:T(128)S(1)}, s32[2]{0:T(128)}, u32[]{:S(2)}) copy-start(s32[2]{0:T(128)} %param.32) | copy-start | bytes 28
  213.3 3.3 %copy-start.8 = (bf16[2,512,512]{2,1,0:T(8,128)(2,1)S(1)}, bf16[2,512,512]{2,1,0:T(8,128)(2,1)}, u32[]{:S(2)}) copy-start(bf16[2,512,512]{2,1,0:T(8,128)(2,1)} %param.31) | copy-start | bytes 3145732
  213.3 3.6 %copy-start.17 = (bf16[64,512]{1,0:T(8,128)(2,1)S(1)}, bf16[64,512]{1,0:T(8,128)(2,1)}, u32[]{:S(2)}) copy-start(bf16[64,512]{1,0:T(8,128)(2,1)} %param.34) | copy-start | bytes 196612
  213.4 4.4 %copy-start.20 = (pred[64]{0:T(512)(128)(4,1)S(1)}, pred[64]{0:T(512)(128)(4,1)}, u32[]{:S(2)}) copy-start(pred[64]{0:T(512)(128)(4,1)} %copy-done.19) | copy-start | bytes 196
  (2 other events, 1.6 us)
Sparse Core Ops, SparseCore 0:
  10.2 83.7 all-gather.1
  213.5 50.9 reduce-scatter.1
where the time goes:
time: 276 us; the launch traced here: 275 us
  Pallas kernels  174 us (63%)
  other arithmetic  42.1 us (15%)
  waiting for transfers between devices  29.3 us (11%)
  between operations  14.5 us (5%)
  local copies, waits for them, and re-layouts  8.83 us (3%)
  matrix products  6.46 us (2%)
    pallas_call x1, Pallas kernels, gather_project(): pl.pallas_call(functools.partial(gather_project_kernel, prompt_rows=promp...  148 us
    reduce_scatter x1, waiting for transfers between devices, on_device(): lax.psum_scatter(partial_sum, 'head', scatter_dimension=1, tiled=True)  29.3 us
    pallas_call x1, Pallas kernels, recurrence(): pl.pallas_call(functools.partial(recurrence_kernel, breadth=breadth, span...  25.7 us
    select_n x1, other arithmetic, on_device(): jnp.where(slot_hit[:, None, None, None], final_state[prompt_index], new_s...  17.5 us
    reduce_sum x1, other arithmetic, on_device(): jnp.sum(slot_r[..., None] * begin_state, axis=2)  7.96 us
    dot_general x1, matrix products, project(): return jnp.dot(left, right, preferred_element_type=jnp.float32)  6.46 us
  transfers between devices with their start and end apart: 2, of which 1 were waited for; matrix products, arithmetic and copies ran while one was open for 16% of the time, Pallas kernels for 63%

commit v1 on v0

--- a/solution.py
+++ b/solution.py
@@ -379,11 +379,13 @@
             final_ref[0, 2 * index + 1] = turned[breadth:, breadth:]
 
 
-def recurrence(r, k, v, w, g, reward, gain, offset, prompt_count, length, breadth):
+def recurrence(r, k, v, w, g, reward, gain, offset, prompt, length, breadth):
+    prompt_count = 1
     columns = r.shape[1]
     span = min(128, length)
     chunks = length // span
-    rows_spec = pl.BlockSpec((span, columns), lambda p, c: (p * chunks + c, 0))
+    rows_spec = pl.BlockSpec((span, columns), lambda p, c: (prompt * chunks + c, 0))
+    out_spec = pl.BlockSpec((span, columns), lambda p, c: (c, 0))
     vector_spec = pl.BlockSpec((1, columns), lambda p, c: (0, 0))
     heads = columns // breadth
     return pl.pallas_call(
@@ -395,7 +397,7 @@
         ),
         in_specs=[rows_spec] * 5 + [vector_spec] * 3,
         out_specs=(
-            rows_spec,
+            out_spec,
             pl.BlockSpec((1, heads, breadth, breadth), lambda p, c: (p, 0, 0, 0)),
         ),
         scratch_shapes=[pltpu.VMEM((heads // 2, 2 * breadth, 2 * breadth), jnp.float32)],
@@ -483,19 +485,40 @@
         length,
         lax.axis_size("req"),
     )
-    gated_prompts, final_state = recurrence(
-        acceptance,
-        address,
-        content,
-        log_decay,
-        gates,
-        current_reward.reshape(1, -1),
-        gain,
-        offset,
-        prompt_count,
-        length,
-        group_breadth,
-    )
+    offsets = request_destination_place - lax.axis_index("req") * slot_count
+    slot_ids = lax.broadcasted_iota(jnp.int32, (slot_count,), 0)
+    prompt_taken = jnp.zeros((slot_count,), jnp.bool_)
+    for prompt_index in range(prompt_count):
+        prompt_taken = prompt_taken | (slot_ids == offsets[prompt_index])
+
+    def prompt_rows_of(prompt_index, gain):
+        return recurrence(
+            acceptance,
+            address,
+            content,
+            log_decay,
+            gates,
+            current_reward.reshape(1, -1),
+            gain,
+            offset,
+            prompt_index,
+            length,
+            group_breadth,
+        )
+
+    def product(gated, keep):
+        return (project(gated, w_output) * keep).astype(jnp.bfloat16)
+
+    def reduced(partial_sum):
+        return lax.psum_scatter(partial_sum, "head", scatter_dimension=1, tiled=True)
+
+    hidden, final_state = [], []
+    for prompt_index in range(prompt_count - 1):
+        gated, state = prompt_rows_of(prompt_index, gain)
+        final_state.append(state[0])
+        partial_sum = product(gated, live_mask[prompt_index * length : (prompt_index + 1) * length])
+        partial_sum, gain = lax.optimization_barrier((partial_sum, gain))
+        hidden.append(reduced(partial_sum))
 
     def slot_heads(array):
         return array[prompt_rows:].astype(jnp.float32).reshape(-1, owned_groups, group_breadth)
@@ -503,6 +526,9 @@
     slot_r, slot_k, slot_v, slot_w = [
         slot_heads(array) for array in (acceptance, address, content, log_decay)
     ]
+    slot_r, slot_k, slot_v, slot_w, gain = lax.optimization_barrier(
+        (slot_r, slot_k, slot_v, slot_w, gain)
+    )
     group_reward = current_reward.reshape(owned_groups, group_breadth)
     begin_state = jnp.where(fresh_mask[:, None, None, None], 0.0, place_memory_matrix)
     decode_out = (
@@ -511,37 +537,33 @@
     )
     normed_slots = group_norm(decode_out, group_scaling_factor, group_scaling_offset)
     gated_slots = (normed_slots * gates[prompt_rows:]).astype(jnp.bfloat16)
-    partial_sum = project(jnp.concatenate([gated_prompts, gated_slots]), w_output).astype(
-        jnp.bfloat16
-    )
+    gated, state = prompt_rows_of(prompt_count - 1, gain)
+    final_state.append(state[0])
+    if hidden:
+        gated, hidden[-1] = lax.optimization_barrier((gated, hidden[-1]))
+    keep = jnp.concatenate(
+        [live_mask[prompt_rows - length :], jnp.where(prompt_taken, 0.0, 1.0)[:, None]]
+    )
+    partial_sum = product(jnp.concatenate([gated, gated_slots]), keep)
     partial_sum, slot_k, slot_v, slot_w = lax.optimization_barrier(
         (partial_sum, slot_k, slot_v, slot_w)
     )
-    hidden = lax.psum_scatter(partial_sum, "head", scatter_dimension=1, tiled=True)
+    last = reduced(partial_sum)
+    hidden.append(last[:length])
+    decode_hidden = last[length:]
+    prompt_hidden = jnp.stack(hidden)
     new_state = (
         jnp.exp(slot_w)[..., None] * begin_state + slot_k[..., :, None] * slot_v[..., None, :]
-    )
-    prompt_hidden = (
-        (hidden[:prompt_rows].astype(jnp.float32) * live_mask)
-        .astype(jnp.bfloat16)
-        .reshape(prompt_count, length, block_cols)
     )
     select = (positions == request_valid_count[:, None] - 1).astype(jnp.float32)
     last_tokens = jnp.sum(
         request_hidden_entries.astype(jnp.float32) * select[..., None], axis=1
     ).astype(jnp.bfloat16)
-    offsets = request_destination_place - lax.axis_index("req") * slot_count
-    slot_ids = lax.broadcasted_iota(jnp.int32, (slot_count,), 0)
     new_shift = newest_symbol_hidden
-    prompt_taken = jnp.zeros((slot_count,), jnp.bool_)
     for prompt_index in range(prompt_count):
         slot_hit = slot_ids == offsets[prompt_index]
         new_state = jnp.where(slot_hit[:, None, None, None], final_state[prompt_index], new_state)
         new_shift = jnp.where(slot_hit[:, None], last_tokens[prompt_index], new_shift)
-        prompt_taken = prompt_taken | slot_hit
-    decode_hidden = jnp.where(
-        prompt_taken[:, None], jnp.zeros((), jnp.bfloat16), hidden[prompt_rows:]
-    )
     return (prompt_hidden, decode_hidden, new_state, new_shift)
 
 

time: 276 us -> 272 us (0.986)
  waiting for transfers between devices: 29.3 us -> 17.6 us
    reduce_scatter x1 -> x2, waiting for transfers between devices: 29.3 us -> 17.6 us  [reduced(): lax.psum_scatter(partial_sum, 'head', scatter_dimension=1, tiled=True)]
    convert_element_type x2 -> x0, other arithmetic: 3.33 us -> none  [the longest x1 2.48 us: on_device(): prompt_hidden = (hidden[:prompt_rows].astype(jnp.float32) * live_mask).as...]
    mul x1, other arithmetic: 0.85 us -> 3.74 us  [on_device(): jnp.sum(slot_r * group_reward * slot_k, axis=-1, keepdims=True) * slot_v]
    dot_general x1 -> x2, matrix products: 6.46 us -> 8.66 us  [project(): return jnp.dot(left, right, preferred_element_type=jnp.float32)]
    pallas_call x1 -> x2, Pallas kernels: 25.7 us -> 26.5 us  [recurrence(): pl.pallas_call(functools.partial(recurrence_kernel, breadth=breadth, span...]
  transfers between devices with their start and end apart: 2 -> 3, of which waited for: 1 -> 2; matrix products, arithmetic and copies ran while one was open for 16% -> 17% of each run, Pallas kernels for 63% -> 65%
where the time goes in v1:
time: 272 us; the launch traced here: 271 us
  Pallas kernels  176 us (65%)
  other arithmetic  44.6 us (16%)
  waiting for transfers between devices  17.6 us (6%)
  between operations  14.2 us (5%)
  local copies, waits for them, and re-layouts  9.64 us (4%)
  matrix products  8.66 us (3%)
    pallas_call x1, Pallas kernels, gather_project(): pl.pallas_call(functools.partial(gather_project_kernel, prompt_rows=promp...  149 us
    pallas_call x2, Pallas kernels, recurrence(): pl.pallas_call(functools.partial(recurrence_kernel, breadth=breadth, span...  26.5 us
    select_n x1, other arithmetic, on_device(): jnp.where(slot_hit[:, None, None, None], final_state[prompt_index], new_s...  17.6 us
    reduce_scatter x2, waiting for transfers between devices, reduced(): lax.psum_scatter(partial_sum, 'head', scatter_dimension=1, tiled=True)  17.6 us
    dot_general x2, matrix products, project(): return jnp.dot(left, right, preferred_element_type=jnp.float32)  8.66 us
    reduce_sum x1, other arithmetic, on_device(): jnp.sum(slot_r[..., None] * begin_state, axis=2)  8.61 us
  transfers between devices with their start and end apart: 3, of which 2 were waited for; matrix products, arithmetic and copies ran while one was open for 17% of the time, Pallas kernels for 65%

profile of v1, /device:TPU:0, one launch (start us, length us, event | category | flops | bytes accessed | tf_op | source)
XLA Modules:
  0.0 270.9 jit_solution(6840771039816612230)
XLA Ops:
  7.3 1.9 convert_element_type.58
  9.2 1.1 convert_element_type.56
  10.3 1.1 convert_element_type.55
  13.5 1.1 pad_maximum_fusion.features_ref
  14.6 149.4 %shard_map.210 = (bf16[1088,512]{1,0:T(8,128)(2,1)S(1)}, bf16[1088,512]{1,0:T(8,128)(2,1)}, bf16[1088,512]{1,0:T(8,128)(2,1)}, f32[1088,512]{1,0:T(8,128)}, f32[1088,512]{1,0:T(8,128)}) custom-call(bf16[1152,512]{1,0:T(8,128)(2,1)} %pad_maximum_fusion.features_ref, bf16[4,4,64,512]{3,2,1,0:T(8,128)(2,1)S(1)} %pad_maximum_fusion.1.shards_ref, ...), custom_call_target="tpu_custom_call" | custom-call | flops 9126805504 | bytes 209715200 | tf_op jit(solution)/shard_map/pallas_call | solution.py:265
  164.1 1.2 copy-done
  165.3 13.2 %shard_map.211 = (bf16[512,512]{1,0:T(8,128)(2,1)S(1)}, f32[1,8,64,64]{3,2,1,0:T(8,128)S(1)}) custom-call(bf16[1088,512]{1,0:T(8,128)(2,1)S(1)} %copy-done, bf16[1088,512]{1,0:T(8,128)(2,1)S(1)} %get-tuple-element.27.k_ref, bf16[1088,512]{1,0:T(8,128)(2,1)} %get-tuple-element.28.v_ref, f32[1088,512]{1,0:T(8,128)} %get-tuple-element.29.w_ref, ...), custom_call_target="tpu_custom_call" | custom-call | flops 671088640 | bytes 3670016 | tf_op jit(solution)/shard_map/pallas_call | solution.py:391
  179.1 4.2 %multiply_convert_fusion.1 = bf16[512,2048]{1,0:T(8,128)(2,1)} fusion(bf16[512,512]{1,0:T(8,128)(2,1)S(1)} %get-tuple-element.31, bf16[512,2048]{1,0:T(8,128)(2,1)} %all-gather.2.cloned.1.call-done, f32[512]{0:T(512)S(1)} %bitcast.70), kind=kOutput, calls=%fused_computation.4 | convolution fusion | flops 1075838976 | bytes 4720640 | tf_op jit(solution)/shard_map/dot_general | solution.py:15
  183.6 1.0 slice.48
  184.9 0.9 slice_convert_fusion
  188.0 1.3 or_select_fusion
  189.3 1.3 maximum_reduce_fusion
  190.6 8.6 %multiply_reduce_fusion = f32[64,8,64]{2,1,0:T(8,128)S(1)} fusion(f32[64,8,64,64]{3,2,1,0:T(8,128)} %param.36, f32[64,8,64]{2,1,0:T(8,128)S(1)} %reshape.192, pred[64]{0:T(512)(128)(4,1)} %copy-done.21), kind=kLoop, calls=%fused_computation.2 | loop fusion | flops 6258688 | bytes 8650816 | tf_op jit(solution)/shard_map/reduce_sum | solution.py:535
  199.2 3.7 %fusion.12 = (f32[64,8]{1,0:T(8,128)S(1)}, f32[64,8,64]{2,1,0:T(8,128)S(1)}) fusion(f32[64,8,64]{2,1,0:T(8,128)S(1)} %multiply_reduce_fusion, f32[64,8,64]{2,1,0:T(8,128)S(1)} %reshape.196, f32[64,8,64]{2,1,0:T(8,128)S(1)} %reshape.194, f32[64,8,64]{2,1,0:T(8,128)S(1)} %reshape.192, f32[8,64]{1,0:T(8,128)S(1)} %mul.100), kind=kOutput, calls=%fused_computation.49 | output fusion | flops 163903 | bytes 659456 | tf_op jit(solution)/shard_map/mul | solution.py:536
  204.2 13.3 %shard_map.212 = (bf16[512,512]{1,0:T(8,128)(2,1)S(1)}, f32[1,8,64,64]{3,2,1,0:T(8,128)S(1)}) custom-call(bf16[1088,512]{1,0:T(8,128)(2,1)S(1)} %copy-done.1, bf16[1088,512]{1,0:T(8,128)(2,1)S(1)} %get-tuple-element.27.k_ref, bf16[1088,512]{1,0:T(8,128)(2,1)} %get-tuple-element.28.v_ref, f32[1088,512]{1,0:T(8,128)} %get-tuple-element.29.w_ref, ...), custom_call_target="tpu_custom_call" | custom-call | flops 671088640 | bytes 3670016 | tf_op jit(solution)/shard_map/pallas_call | solution.py:391
  217.5 0.9 multiply_convert_fusion.2
  218.4 1.5 reduce-scatter.3.cloned.1.call-done
  219.9 4.4 %multiply_convert_fusion = bf16[576,2048]{1,0:T(8,128)(2,1)} fusion(bf16[512,2048]{1,0:T(8,128)(2,1)} %all-gather.2.cloned.1.call-done, f32[576]{0:T(1024)S(1)} %copy-done.23, bf16[64,512]{1,0:T(8,128)(2,1)S(1)} %multiply_convert_fusion.2, bf16[512,512]{1,0:T(8,128)(2,1)S(1)} %get-tuple-element.37), kind=kOutput, calls=%fused_computation.3 | convolution fusion | flops 1211498496 | bytes 5048576 | tf_op jit(solution)/shard_map/dot_general | solution.py:15
  224.4 1.4 iota_compare_fusion.1
  227.1 17.6 %select_select_fusion = f32[64,8,64,64]{3,2,1,0:T(8,128)} fusion(f32[64,8,64,64]{3,2,1,0:T(8,128)} %param.36, f32[64,8,64]{2,1,0:T(8,128)S(1)} %copy-done.10, f32[64,8,64]{2,1,0:T(8,128)S(1)} %reshape.194, f32[64,8,64]{2,1,0:T(8,128)S(1)} %exp.3, f32[8,64,64]{2,1,0:T(8,128)S(1)} %bitcast.53, f32[8,64,64]{2,1,0:T(8,128)S(1)} %bitcast.54, ...), kind=kLoop, calls=%fused_computation.1 | loop fusion | flops 12582912 | bytes 17432768 | tf_op jit(solution)/shard_map/jit(_where)/select_n | solution.py:565
  244.7 16.1 %reduce-scatter.5.cloned.1.call-done = bf16[576,512]{1,0:T(8,128)(2,1)} async-done(((bf16[576,2048]{1,0:T(8,128)(2,1)}), bf16[576,512]{1,0:T(8,128)(2,1)}) %reduce-scatter.5.cloned.1.call-update) | async-done | bytes 589840 | tf_op jit(solution)/shard_map/reduce_scatter | solution.py:513
  260.8 1.1 slice_bitcast_fusion
  261.9 1.1 pad_maximum_fusion.2
  262.9 1.5 slice.62
  (94 shorter events, 7.8 us)
Async XLA Ops:
  7.2 4.2 %copy-start.12 = (f32[64,2048]{1,0:T(8,128)S(1)}, f32[64,2048]{1,0:T(8,128)}, u32[]{:S(2)}) copy-start(f32[64,2048]{1,0:T(8,128)} %param.21) | copy-start | bytes 1572868
  7.2 4.2 %copy-start.13 = (f32[64,2048]{1,0:T(8,128)S(1)}, f32[64,2048]{1,0:T(8,128)}, u32[]{:S(2)}) copy-start(f32[64,2048]{1,0:T(8,128)} %param.20) | copy-start | bytes 1572868
  7.2 4.3 %copy-start.20 = (f32[5,2048]{1,0:T(8,128)S(1)}, f32[5,2048]{1,0:T(8,128)}, u32[]{:S(2)}) copy-start(f32[5,2048]{1,0:T(8,128)} %param.28) | copy-start | bytes 122884
  7.2 4.3 %copy-start.16 = (bf16[2048,64]{0,1:T(8,128)(2,1)S(1)}, bf16[2048,64]{0,1:T(8,128)(2,1)}, u32[]{:S(2)}) copy-start(bf16[2048,64]{0,1:T(8,128)(2,1)} %param.24) | copy-start | bytes 786436
  7.2 4.6 %copy-start.24 = (s32[2]{0:T(128)S(1)}, s32[2]{0:T(128)}, u32[]{:S(2)}) copy-start(s32[2]{0:T(128)} %param.32) | copy-start | bytes 28
  7.2 171.9 %all-gather.2.cloned.1.call-start = ((), (), s32[]{:S(2)}) async-start(), calls=%async_computation.2 | async-start | bytes 2359296 | tf_op jit(solution)/shard_map/all_gather | solution.py:467
  9.2 210.8 %reduce-scatter.3.cloned.1.call-start = ((), (), s32[]{:S(2)}) async-start(), calls=%async_computation.3 | async-start | bytes 2621440 | tf_op jit(solution)/shard_map/reduce_scatter | solution.py:513
  12.3 2.2 copy-start.5
  12.4 2.2 copy-start.6
  12.7 1.9 copy-start.21
  14.6 149.5 %copy-start.2 = (f32[512]{0:T(512)S(1)}, f32[512]{0:T(512)}, u32[]{:S(2)}) copy-start(f32[512]{0:T(512)} %param.27) | copy-start | bytes 6148
  14.6 149.5 %copy-start.3 = (f32[512]{0:T(512)S(1)}, f32[512]{0:T(512)}, u32[]{:S(2)}) copy-start(f32[512]{0:T(512)} %param.29) | copy-start | bytes 6148
  14.6 149.5 %copy-start.4 = (f32[512]{0:T(512)S(1)}, f32[512]{0:T(512)}, u32[]{:S(2)}) copy-start(f32[512]{0:T(512)} %param.30) | copy-start | bytes 6148
  183.4 77.4 %reduce-scatter.5.cloned.1.call-start = ((), (), s32[]{:S(2)}) async-start(), calls=%async_computation.4 | async-start | bytes 2949120 | tf_op jit(solution)/shard_map/reduce_scatter | solution.py:513
  185.9 13.3 %copy-start.9 = (f32[64,8,64]{2,1,0:T(8,128)}, f32[64,8,64]{2,1,0:T(8,128)S(1)}, u32[]{:S(2)}) copy-start(f32[64,8,64]{2,1,0:T(8,128)S(1)} %reshape.196) | copy-start | bytes 393220
  204.2 13.3 %copy-start.14 = (f32[64,512]{1,0:T(8,128)S(1)}, f32[64,512]{1,0:T(8,128)}, u32[]{:S(2)}) copy-start(f32[64,512]{1,0:T(8,128)} %reshape.190) | copy-start | bytes 393220
  204.2 15.7 %copy-start.23 = (f32[576]{0:T(1024)S(1)}, f32[576]{0:T(1024)}, u32[]{:S(2)}) copy-start(f32[576]{0:T(1024)} %maximum_reduce_fusion) | copy-start | bytes 6916
  224.4 1.5 copy-start.25
  224.4 1.6 copy-start.8
  224.4 1.9 copy-start.18
  224.4 2.6 copy-start.11
  224.4 2.7 copy-start.10
  224.4 2.7 copy-start.22
  227.1 34.8 %copy-start.15 = (bf16[512,512]{1,0:T(8,128)(2,1)S(1)}, bf16[512,512]{1,0:T(8,128)(2,1)}, u32[]{:S(2)}) copy-start(bf16[512,512]{1,0:T(8,128)(2,1)} %reduce-scatter.3.cloned.1.call-done) | copy-start | bytes 1572868
  (6 other events, 6.6 us)
Sparse Core Ops, SparseCore 0:
  10.8 88.6 all-gather.1
  183.5 36.3 reduce-scatter.2
  224.6 36.1 reduce-scatter.4
